TPU v7x, 32 devices: a whole 2x2x4 slice. The times are simulated.
32 devices in a mesh: groups: 2 (over y), seq: 4 (over z), head: 2 (over x), tp: 2 (over core).
Axes of the slice: x: 2, y: 2, z: 4, core: 2. Of those that a mesh axis runs over, the one named last changes fastest.
Arguments:
- ssm_input: bfloat16 [2048, 8192], P(('groups', 'seq'), ('head', 'tp')), parts along dimension 0, may hold values from -6 to 6
- ssm_gate: bfloat16 [2048, 8192], P(('groups', 'seq'), ('head', 'tp')), parts along dimension 0, may hold values from -6 to 6
- input_map: bfloat16 [2048, 512], P(('groups', 'seq'), ('head', 'tp')), parts along dimension 0, may hold values from -0.5 to 0.5
- output_map: bfloat16 [2048, 512], P(('groups', 'seq'), ('head', 'tp')), parts along dimension 0, may hold values from -6 to 6
- step_size: float32 [128, 2048], P(('head', 'tp'), ('groups', 'seq')), parts along dimension 1, may hold values from 0.5 to 2
- decay_log: float32 [128], P(('head', 'tp')), may hold values from -16 to -2
- skip_gain: float32 [128], P(('head', 'tp')), may hold values from 0.5 to 1.5
- norm_gain: float32 [8192], P(('head', 'tp')), may hold values from 0.25 to 1.75
- doc_lengths: int32 [8], P('groups'), parts along dimension 0, may hold values from 1 to 512, 1024 in all
- queries: bfloat16 [2048, 4096], P(('groups', 'seq', 'head'), 'tp'), parts along dimension 0, may hold values from -64 to 64
- keys_in: bfloat16 [2048, 1024], P(('groups', 'seq', 'head'), 'tp'), parts along dimension 0, may hold values from -16 to 16
- values_in: bfloat16 [2048, 1024], P(('groups', 'seq', 'head'), 'tp'), parts along dimension 0, may hold values from -6 to 6
Outputs:
- ssm_out: bfloat16 [2048, 8192], P(('groups', 'seq'), ('head', 'tp')), parts along dimension 0
- attn_out: bfloat16 [2048, 4096], P(('groups', 'seq', 'head'), 'tp'), parts along dimension 0
There are 2 independent parts, one for each index of `groups`. A program takes and returns all parts, laid end to end along the dimension named above; an argument that names none is the same for every part. Nothing has to cross between parts.
Inputs may be any that keep to these rules, and one draw needn't show every extreme that they name: `doc_lengths`: the 4 documents lie end to end from position 0; their lengths sum to 1024.
All inputs are finite; a program needn't handle non-finite values.
Results may differ from a plain program's by a relative error of at most 0.0052.
Values may be sent and summed in bfloat16 or wider, within the bound.
A program may use at most 128 MiB of HBM per device.

v0:
```python
import math

import jax
import jax.numpy as jnp
from jax import lax
from jax.sharding import PartitionSpec as P

HEAD_P = 64
HEAD_D = 128
REACH = 2


def carried_in(shard, axis, combine, identity):
    count, mine = (lax.axis_size(axis), lax.axis_index(axis))
    everything = jax.tree.map(lambda part: lax.all_gather(part, axis), shard)
    start = jax.tree.map(
        lambda part, zero: jnp.broadcast_to(jnp.asarray(zero, part.dtype), part.shape),
        shard,
        identity,
    )

    def hop(k, before):
        reached = k < mine
        new = combine(before, jax.tree.map(lambda part: part[k], everything))
        return jax.tree.map(lambda a, b: jnp.where(reached, a, b), new, before)

    return lax.fori_loop(0, count, hop, start)


def from_behind(shard, axis, by):
    count = lax.axis_size(axis)
    pairs = [(i, i + by) for i in range(count) if 0 <= i + by < count]
    return lax.ppermute(shard, axis, pairs)


def doc_starts(doc_lengths):
    return jnp.cumsum(doc_lengths) - doc_lengths


def segment_of(starts, positions):
    return jnp.sum((starts[None, :] <= positions[:, None]).astype(jnp.int32), axis=1) - 1


def link_states(earlier, later):
    return (earlier[0] * later[0], later[1] + later[0][:, None, None] * earlier[1])


def attend(queries, keys, values, query_first, key_first, starts):
    query_count = queries.shape[0]
    key_count = keys.shape[0]
    query_heads = queries.shape[1] // HEAD_D
    group_size = query_heads // (keys.shape[1] // HEAD_D)
    query_pos = query_first + jnp.arange(query_count, dtype=jnp.int32)
    key_pos = key_first + jnp.arange(key_count, dtype=jnp.int32)
    allowed = segment_of(starts, query_pos)[:, None] == segment_of(starts, key_pos)[None, :]
    allowed = allowed & (key_pos[None, :] <= query_pos[:, None]) & (key_pos[None, :] >= 0)

    def one_head(head_index):
        query_part = lax.dynamic_slice_in_dim(queries, head_index * HEAD_D, HEAD_D, 1)
        column = head_index // group_size * HEAD_D
        key_part = lax.dynamic_slice_in_dim(keys, column, HEAD_D, 1)
        value_part = lax.dynamic_slice_in_dim(values, column, HEAD_D, 1)
        logits = jnp.einsum(
            "td,sd->ts", query_part, key_part, preferred_element_type=jnp.float32
        ) * (1.0 / math.sqrt(HEAD_D))
        masked = jnp.where(allowed, logits, -jnp.inf)
        highest = jnp.max(masked, axis=1, keepdims=True)
        probs = jnp.where(allowed, jnp.exp(masked - highest), 0.0)
        denominator = jnp.sum(probs, axis=1, keepdims=True)
        mixed = (
            jnp.dot(probs.astype(jnp.bfloat16), value_part, preferred_element_type=jnp.float32)
            / denominator
        )
        return mixed.astype(jnp.bfloat16)

    stacked = lax.map(one_head, jnp.arange(query_heads, dtype=jnp.int32))
    return jnp.transpose(stacked, (1, 0, 2)).reshape(query_count, query_heads * HEAD_D)


def mamba_mixer(
    ssm_input, ssm_gate, input_map, output_map, step_size, decay_log, skip_gain, norm_gain, starts
):
    row_count = ssm_input.shape[0]
    head_count = step_size.shape[0]
    first_row = lax.axis_index("seq") * row_count
    positions = first_row + jnp.arange(row_count, dtype=jnp.int32)
    segment_ids = segment_of(starts, positions)
    segment_before = jnp.sum((starts <= first_row - 1).astype(jnp.int32)) - 1
    cumulative = jnp.cumsum(step_size * (-jnp.exp(decay_log))[:, None], axis=1)
    intersection = jnp.einsum(
        "tn,sn->ts", output_map, input_map, preferred_element_type=jnp.float32
    )
    same_doc = (segment_ids[:, None] == segment_ids[None, :]) & (
        positions[:, None] >= positions[None, :]
    )

    def head_intra(head_index):
        cum_head = cumulative[head_index]
        steps_head = step_size[head_index]
        differences = cum_head[:, None] - cum_head[None, :]
        weights = jnp.where(
            same_doc,
            jnp.exp(jnp.where(same_doc, differences, 0.0)) * intersection * steps_head[None, :],
            0.0,
        )
        inputs_head = lax.dynamic_slice_in_dim(ssm_input, head_index * HEAD_P, HEAD_P, 1)
        return jnp.dot(
            weights.astype(jnp.bfloat16), inputs_head, preferred_element_type=jnp.float32
        )

    intra = jnp.transpose(lax.map(head_intra, jnp.arange(head_count, dtype=jnp.int32)), (1, 0, 2))
    head_inputs = ssm_input.reshape(row_count, head_count, HEAD_P)
    tail_weights = jnp.where(
        (segment_ids == segment_ids[-1])[None, :],
        jnp.exp(cumulative[:, -1:] - cumulative) * step_size,
        0.0,
    )
    scaled_input = (
        jnp.transpose(tail_weights)[:, :, None] * head_inputs.astype(jnp.float32)
    ).astype(jnp.bfloat16)
    local_state = jnp.einsum(
        "sn,shp->hnp", input_map, scaled_input, preferred_element_type=jnp.float32
    )
    any_start = jnp.any((starts >= first_row) & (starts < first_row + row_count))
    factor = jnp.where(any_start, 0.0, jnp.exp(cumulative[:, -1]))
    identity = (jnp.ones_like(factor), jnp.zeros_like(local_state))
    incoming = carried_in((factor, local_state), "seq", link_states, identity)[1]
    inbound = incoming.astype(jnp.bfloat16)
    inter = jnp.einsum("tn,hnp->thp", output_map, inbound, preferred_element_type=jnp.float32)
    reach_scale = jnp.where((segment_ids == segment_before)[None, :], jnp.exp(cumulative), 0.0)
    inter = inter * jnp.transpose(reach_scale)[:, :, None]
    combined = intra + inter + skip_gain[None, :, None] * head_inputs.astype(jnp.float32)
    gated = combined.reshape(row_count, head_count * HEAD_P) * jax.nn.silu(
        ssm_gate.astype(jnp.float32)
    )
    normed = gated * lax.rsqrt(jnp.mean(gated * gated, axis=1, keepdims=True) + 1e-05)
    return (normed * norm_gain[None, :]).astype(jnp.bfloat16)


def on_device(
    ssm_input,
    ssm_gate,
    input_map,
    output_map,
    step_size,
    decay_log,
    skip_gain,
    norm_gain,
    doc_lengths,
    queries,
    keys_in,
    values_in,
):
    starts = doc_starts(doc_lengths)
    ssm_out = mamba_mixer(
        ssm_input,
        ssm_gate,
        input_map,
        output_map,
        step_size,
        decay_log,
        skip_gain,
        norm_gain,
        starts,
    )
    moved_queries, moved_keys, moved_values = (
        lax.all_to_all(queries, "head", split_axis=1, concat_axis=0, tiled=True),
        lax.all_to_all(keys_in, "head", split_axis=1, concat_axis=0, tiled=True),
        lax.all_to_all(values_in, "head", split_axis=1, concat_axis=0, tiled=True),
    )
    block_rows = moved_queries.shape[0]
    first_query = lax.axis_index("seq") * block_rows
    key_parts = [moved_keys]
    value_parts = [moved_values]
    for distance in range(1, REACH + 1):
        before_keys, before_values = from_behind((moved_keys, moved_values), "seq", distance)
        key_parts = [before_keys] + key_parts
        value_parts = [before_values] + value_parts
    all_keys = jnp.concatenate(key_parts, axis=0)
    all_values = jnp.concatenate(value_parts, axis=0)
    mixed = attend(
        moved_queries, all_keys, all_values, first_query, first_query - REACH * block_rows, starts
    )
    attn_out = lax.all_to_all(mixed, "head", split_axis=0, concat_axis=1, tiled=True)
    return (ssm_out, attn_out)


def solution(mesh):
    placed = (
        P(("groups", "seq"), ("head", "tp")),
        P(("groups", "seq"), ("head", "tp")),
        P(("groups", "seq"), ("head", "tp")),
        P(("groups", "seq"), ("head", "tp")),
        P(("head", "tp"), ("groups", "seq")),
        P(("head", "tp")),
        P(("head", "tp")),
        P(("head", "tp")),
        P("groups"),
        P(("groups", "seq", "head"), "tp"),
        P(("groups", "seq", "head"), "tp"),
        P(("groups", "seq", "head"), "tp"),
    )
    return jax.shard_map(
        on_device,
        mesh=mesh,
        in_specs=placed,
        out_specs=(P(("groups", "seq"), ("head", "tp")), P(("groups", "seq", "head"), "tp")),
        check_vma=False,
    )
```

profile of v0, /device:TPU:0, one launch (start us, length us, event | category | flops | bytes accessed | tf_op | source)
XLA Modules:
  0.0 333.8 jit_solution(6185780756927128226)
XLA Ops:
  19.1 4.2 %all-to-all-start.1 = ((bf16[128,2,256]{2,0,1:T(8,128)(2,1)}), bf16[128,2,256]{2,0,1:T(8,128)(2,1)S(1)}, u32[]{:S(2)}, u32[]{:S(2)}) async-start(bf16[128,2,256]{2,0,1:T(8,128)(2,1)} %bitcast.87), calls=%async_computation.1 | async-start | bytes 262144 | tf_op jit(solution)/shard_map/all_to_all | solution.py:168
  24.3 3.6 %all-to-all-done.1 = bf16[128,2,256]{2,0,1:T(8,128)(2,1)S(1)} async-done(((bf16[128,2,256]{2,0,1:T(8,128)(2,1)}), bf16[128,2,256]{2,0,1:T(8,128)(2,1)S(1)}, u32[]{:S(2)}, u32[]{:S(2)}) %all-to-all-start.1) | async-done | bytes 131104 | tf_op jit(solution)/shard_map/all_to_all | solution.py:168
  27.9 3.4 %all-to-all-start.2 = ((bf16[128,2,256]{2,0,1:T(8,128)(2,1)}), bf16[128,2,256]{2,0,1:T(8,128)(2,1)S(1)}, u32[]{:S(2)}, u32[]{:S(2)}) async-start(bf16[128,2,256]{2,0,1:T(8,128)(2,1)} %bitcast.86), calls=%async_computation.2 | async-start | bytes 262144 | tf_op jit(solution)/shard_map/all_to_all | solution.py:169
  31.3 5.0 %collective-permute-start = (bf16[256,256]{1,0:T(8,128)(2,1)S(1)}, bf16[256,256]{1,0:T(8,128)(2,1)S(1)}, u32[]{:S(2)}, u32[]{:S(2)}) collective-permute-start(bf16[256,256]{1,0:T(8,128)(2,1)S(1)} %bitcast.113), channel_id=1, source_target_pairs={{0,8},{4,12},{1,9},{5,13},{2,10},{6,14},{3,11},{7,15},{16,24},{20,... | collective-permute-start | bytes 393224 | tf_op jit(solution)/shard_map/ppermute | solution.py:33
  36.3 3.5 %collective-permute-start.1 = (bf16[256,256]{1,0:T(8,128)(2,1)S(1)}, bf16[256,256]{1,0:T(8,128)(2,1)S(1)}, u32[]{:S(2)}, u32[]{:S(2)}) collective-permute-start(bf16[256,256]{1,0:T(8,128)(2,1)S(1)} %bitcast.114), channel_id=1, source_target_pairs={{0,4},{4,8},{8,12},{1,5},{5,9},{9,13},{2,6},{6,10},{10,14},{3,7},{... | collective-permute-start | bytes 393224 | tf_op jit(solution)/shard_map/ppermute | solution.py:33
  40.7 3.5 %all-to-all-start = ((bf16[128,2,1024]{2,0,1:T(8,128)(2,1)}), bf16[128,2,1024]{2,0,1:T(8,128)(2,1)S(1)}, u32[]{:S(2)}, u32[]{:S(2)}) async-start(bf16[128,2,1024]{2,0,1:T(8,128)(2,1)} %bitcast.85), calls=%async_computation | async-start | bytes 1048576 | tf_op jit(solution)/shard_map/all_to_all | solution.py:167
  45.5 2.3 collective-permute-start.3
  48.6 5.6 %collective-permute-done.2 = bf16[256,256]{1,0:T(8,128)(2,1)S(1)} collective-permute-done((bf16[256,256]{1,0:T(8,128)(2,1)S(1)}, bf16[256,256]{1,0:T(8,128)(2,1)S(1)}, u32[]{:S(2)}, u32[]{:S(2)}) %collective-permute-start.2) | collective-permute-done | bytes 131104 | tf_op jit(solution)/shard_map/ppermute | solution.py:33
  54.2 4.9 %collective-permute-done.3 = bf16[256,256]{1,0:T(8,128)(2,1)S(1)} collective-permute-done((bf16[256,256]{1,0:T(8,128)(2,1)S(1)}, bf16[256,256]{1,0:T(8,128)(2,1)S(1)}, u32[]{:S(2)}, u32[]{:S(2)}) %collective-permute-start.3) | collective-permute-done | bytes 131104 | tf_op jit(solution)/shard_map/ppermute | solution.py:33
  59.1 41.9 %while.39 = (s32[]{:T(128)}, bf16[8,256,128]{2,1,0:T(8,128)(2,1)S(1)}, s32[8]{0:T(128)S(1)}, bf16[256,1024]{1,0:T(8,128)(2,1)S(1)}, bf16[768,256]{1,0:T(8,128)(2...) while((s32[]{:T(128)}, ...), condition=%wide.region_15.16_spmd.clone, body=%wide.region_12.15_spmd.clone.sunk | while | flops 104857112 | bytes 2920635 | solution.py:76
  102.4 3.5 %all-to-all-start.3 = ((bf16[2,128,1024]{2,1,0:T(8,128)(2,1)}), bf16[2,128,1024]{2,1,0:T(8,128)(2,1)S(1)}, u32[]{:S(2)}, u32[]{:S(2)}) async-start(bf16[2,128,1024]{2,1,0:T(8,128)(2,1)} %all_to_all.68), calls=%async_computation.3 | async-start | bytes 1048576 | tf_op jit(solution)/shard_map/all_to_all | solution.py:184
  105.9 157.8 %while.38 = (s32[]{:T(128)}, f32[32,256,64]{1,2,0:T(8,128)}, s32[32]{0:T(128)S(1)}, f32[32,256]{1,0:T(8,128)S(1)}, f32[256,256]{1,0:T(8,128)S(1)}, /*index=5*/f3...) while((s32[]{:T(128)}, f32[32,256,64]{1,2,0:T(8,128)}, ...), condition=%wide.region_5.6_spmd.clone, body=%wide.region_4.5_spmd.clone.sunk | while | flops 8978441 | bytes 405225 | solution.py:111
  109.1 1.8 fusion.56
  114.0 1.8 fusion.56
  133.7 1.8 fusion.56
  143.6 1.8 fusion.56
  153.4 1.8 fusion.56
  158.4 1.8 fusion.56
  173.2 1.8 fusion.56
  178.1 1.8 fusion.56
  183.0 1.8 fusion.56
  188.0 1.8 fusion.56
  247.1 1.8 fusion.56
  261.9 1.8 fusion.56
  265.3 31.3 %all-reduce = f32[128]{0:T(128)S(1)} all-reduce(f32[128]{0:T(128)S(1)} %dynamic-update-slice), channel_id=3, replica_groups=mesh['groups'=2,'seq'=4,'head'=2,'tp'=2] {'seq'}, use_global_device_ids=true, to_apply=%add | all-reduce | flops 128 | bytes 1024
  298.0 19.4 %while.40 = (s32[]{:T(128)}, f32[32,128,64]{2,1,0:T(8,128)}, s32[]{:T(128)}, f32[4,32,128,64]{2,3,1,0:T(8,128)}, f32[4,32]{1,0:T(4,128)S(1)}, /*index=5*/s32[]{:T(128)}, s32[]{:T(128)}) while((s32[]{:T(128)}, f32[32,128,64]{2,1,0:T(8,128)}, s32[]{:T(128)}, f32[4,32,128,64]{2,3,1,0:T(8,128)}, f32[4,32]{1,0:T(4,128)S(1)}, ...), condition=%wide.region_8.9_spmd.clone, body=%wide.region_7.8_spmd.clone.sunk | while | flops 1048580 | bytes 7340521 | solution.py:27
  303.6 3.3 fusion.62
  308.9 3.3 fusion.62
  314.1 3.3 fusion.62
  317.5 4.9 %fusion.37 = f32[256,32,64]{0,2,1:T(8,128)} fusion(f32[32,256,64]{1,2,0:T(8,128)} %get-tuple-element.228, f32[256,32,64]{0,2,1:T(8,128)} %bitcast.105, f32[32]{0:T(128)S(1)} %copy-done.9, f32[256,32]{0,1:T(8,128)S(1)} %get-tuple-element.390, f32[32,128,64]{2,1,0:T(8,128)} %get-tuple-element.229, bf16[256,128]{1,0:T(8,128)(2,1)S(1)} %copy-done), kind=kOutput, calls=%fused_computation.48 | convolution fusion | flops 136577024 | bytes 7438464 | tf_op jit(solution)/shard_map/tn,hnp->thp/dot_general | solution.py:129
  322.4 2.0 copy.61
  325.2 1.8 multiply_convert_fusion
  (204 shorter events, 99.9 us)
Async XLA Ops:
  7.2 16.2 %copy-start = (bf16[256,128]{1,0:T(8,128)(2,1)S(1)}, bf16[256,128]{1,0:T(8,128)(2,1)}, u32[]{:S(2)}) copy-start(bf16[256,128]{1,0:T(8,128)(2,1)} %param.21) | copy-start | bytes 196612
  7.2 9.7 %copy-start.5 = (f32[32,256]{1,0:T(8,128)S(1)}, f32[32,256]{1,0:T(8,128)}, u32[]{:S(2)}) copy-start(f32[32,256]{1,0:T(8,128)} %param.22) | copy-start | bytes 98308
  7.2 9.8 %copy-start.4 = (bf16[256,128]{1,0:T(8,128)(2,1)S(1)}, bf16[256,128]{1,0:T(8,128)(2,1)}, u32[]{:S(2)}) copy-start(bf16[256,128]{1,0:T(8,128)(2,1)} %param.20) | copy-start | bytes 196612
  7.2 290.8 %all-gather.4.cloned.1.call-start = ((), (), s32[]{:S(2)}) async-start(), calls=%async_computation.4 | async-start | bytes 5242880 | tf_op jit(solution)/shard_map/all_gather | solution.py:15
  15.3 3.1 copy-start.1
  17.0 1.5 copy-start.6
  17.0 6.5 %copy-start.7 = (bf16[128,512]{1,0:T(8,128)(2,1)S(1)}, bf16[128,512]{1,0:T(8,128)(2,1)}, u32[]{:S(2)}) copy-start(bf16[128,512]{1,0:T(8,128)(2,1)} %param.29) | copy-start | bytes 393220
  17.0 22.8 %copy-start.3 = (bf16[128,2048]{1,0:T(8,128)(2,1)S(1)}, bf16[128,2048]{1,0:T(8,128)(2,1)}, u32[]{:S(2)}) copy-start(bf16[128,2048]{1,0:T(8,128)(2,1)} %param.27) | copy-start | bytes 1572868
  19.1 8.8 %all-to-all-start.1 = ((bf16[128,2,256]{2,0,1:T(8,128)(2,1)}), bf16[128,2,256]{2,0,1:T(8,128)(2,1)S(1)}, u32[]{:S(2)}, u32[]{:S(2)}) async-start(bf16[128,2,256]{2,0,1:T(8,128)(2,1)} %bitcast.87), calls=%async_computation.1 | async-start | bytes 262144 | tf_op jit(solution)/shard_map/all_to_all | solution.py:168
  27.9 12.8 %all-to-all-start.2 = ((bf16[128,2,256]{2,0,1:T(8,128)(2,1)}), bf16[128,2,256]{2,0,1:T(8,128)(2,1)S(1)}, u32[]{:S(2)}, u32[]{:S(2)}) async-start(bf16[128,2,256]{2,0,1:T(8,128)(2,1)} %bitcast.86), calls=%async_computation.2 | async-start | bytes 262144 | tf_op jit(solution)/shard_map/all_to_all | solution.py:169
  31.3 16.5 %collective-permute-start = (bf16[256,256]{1,0:T(8,128)(2,1)S(1)}, bf16[256,256]{1,0:T(8,128)(2,1)S(1)}, u32[]{:S(2)}, u32[]{:S(2)}) collective-permute-start(bf16[256,256]{1,0:T(8,128)(2,1)S(1)} %bitcast.113), channel_id=1, source_target_pairs={{0,8},{4,12},{1,9},{5,13},{2,10},{6,14},{3,11},{7,15},{16,24},{20,... | collective-permute-start | bytes 393224 | tf_op jit(solution)/shard_map/ppermute | solution.py:33
  36.3 12.2 %collective-permute-start.1 = (bf16[256,256]{1,0:T(8,128)(2,1)S(1)}, bf16[256,256]{1,0:T(8,128)(2,1)S(1)}, u32[]{:S(2)}, u32[]{:S(2)}) collective-permute-start(bf16[256,256]{1,0:T(8,128)(2,1)S(1)} %bitcast.114), channel_id=1, source_target_pairs={{0,4},{4,8},{8,12},{1,5},{5,9},{9,13},{2,6},{6,10},{10,14},{3,7},{... | collective-permute-start | bytes 393224 | tf_op jit(solution)/shard_map/ppermute | solution.py:33
  40.7 18.4 %all-to-all-start = ((bf16[128,2,1024]{2,0,1:T(8,128)(2,1)}), bf16[128,2,1024]{2,0,1:T(8,128)(2,1)S(1)}, u32[]{:S(2)}, u32[]{:S(2)}) async-start(bf16[128,2,1024]{2,0,1:T(8,128)(2,1)} %bitcast.85), calls=%async_computation | async-start | bytes 1048576 | tf_op jit(solution)/shard_map/all_to_all | solution.py:167
  44.2 10.0 %collective-permute-start.2 = (bf16[256,256]{1,0:T(8,128)(2,1)S(1)}, bf16[256,256]{1,0:T(8,128)(2,1)S(1)}, u32[]{:S(2)}, u32[]{:S(2)}) collective-permute-start(bf16[256,256]{1,0:T(8,128)(2,1)S(1)} %bitcast.116), channel_id=1, source_target_pairs={{0,8},{4,12},{1,9},{5,13},{2,10},{6,14},{3,11},{7,15},{16,24},{20,... | collective-permute-start | bytes 393224 | tf_op jit(solution)/shard_map/ppermute | solution.py:33
  45.5 13.6 %collective-permute-start.3 = (bf16[256,256]{1,0:T(8,128)(2,1)S(1)}, bf16[256,256]{1,0:T(8,128)(2,1)S(1)}, u32[]{:S(2)}, u32[]{:S(2)}) collective-permute-start(bf16[256,256]{1,0:T(8,128)(2,1)S(1)} %bitcast.117), channel_id=1, source_target_pairs={{0,4},{4,8},{8,12},{1,5},{5,9},{9,13},{2,6},{6,10},{10,14},{3,7},{... | collective-permute-start | bytes 393224 | tf_op jit(solution)/shard_map/ppermute | solution.py:33
  102.4 194.3 %all-to-all-start.3 = ((bf16[2,128,1024]{2,1,0:T(8,128)(2,1)}), bf16[2,128,1024]{2,1,0:T(8,128)(2,1)S(1)}, u32[]{:S(2)}, u32[]{:S(2)}) async-start(bf16[2,128,1024]{2,1,0:T(8,128)(2,1)} %all_to_all.68), calls=%async_computation.3 | async-start | bytes 1048576 | tf_op jit(solution)/shard_map/all_to_all | solution.py:184
  105.9 157.8 %copy-start.10 = (u32[32]{0:T(128)S(1)}, u32[32]{0:T(128)}, u32[]{:S(2)}) copy-start(u32[32]{0:T(128)} %constant.155) | copy-start | bytes 388
  298.0 19.4 %copy-start.9 = (f32[32]{0:T(128)S(1)}, f32[32]{0:T(128)}, u32[]{:S(2)}) copy-start(f32[32]{0:T(128)} %param.24) | copy-start | bytes 388
  322.3 2.0 copy-start.2
  324.4 0.8 copy-start.8
Sparse Core Ops, SparseCore 0:
  18.6 90.6 all-gather.3
where the time goes:
time: 338 us; the launch traced here: 334 us
  loops' own time  107 us (32%)
  matrix products  71.6 us (21%)
  local copies, waits for them, and re-layouts  41.8 us (12%)
  blocking collectives  31.3 us (9%)
  starting transfers between devices  26.7 us (8%)
  other arithmetic  24.8 us (7%)
  between operations  15.8 us (5%)
  waiting for transfers between devices  14.8 us (4%)
    another operation x1, loops' own time, mamba_mixer(): lax.map(head_intra, jnp.arange(head_count, dtype=jnp.int32))  80.7 us
    dot_general x32, matrix products, head_intra(): jnp.dot(weights.astype(jnp.bfloat16), inputs_head, preferred_element_type...  57.7 us
    unnamed x1, blocking collectives  31.3 us
    another operation x1, loops' own time, attend(): stacked = lax.map(one_head, jnp.arange(query_heads, dtype=jnp.int32))  26.2 us
    dynamic_slice x32, local copies, waits for them, and re-layouts, mamba_mixer(): lax.map(head_intra, jnp.arange(head_count, dtype=jnp.int32))  19.1 us
    ppermute x4, starting transfers between devices, from_behind(): return lax.ppermute(shard, axis, pairs)  12.1 us
    select_n x4, other arithmetic, hop(): return jax.tree.map(lambda a, b: jnp.where(reached, a, b), new, before)  11.7 us
    ppermute x4, waiting for transfers between devices, from_behind(): return lax.ppermute(shard, axis, pairs)  11.2 us
  transfers between devices with their start and end apart: 9, of which 4 were waited for; matrix products, arithmetic and copies ran while one was open for 29% of the time, Pallas kernels for 0%

commit v1 on v0

v1 whole, which is shorter than its diff:
```python
import functools
import math

import jax
import jax.numpy as jnp
from jax import lax
from jax.experimental import pallas as pl
from jax.experimental.pallas import tpu as pltpu
from jax.sharding import PartitionSpec as P

HEAD_P = 64
HEAD_D = 128
REACH = 2
MESH = pl.DeviceIdType.MESH
TILE = 256
F32 = jnp.float32
BF16 = jnp.bfloat16


def dot(a, b):
    return jnp.dot(a, b, preferred_element_type=F32)


def dot_nt(a, b):
    return lax.dot_general(a, b, (((1,), (1,)), ((), ())), preferred_element_type=F32)


def split3(v):
    hi = v.astype(BF16).astype(F32)
    mid = (v - hi).astype(BF16).astype(F32)
    lo = (v - hi - mid).astype(BF16).astype(F32)
    return hi, mid, lo


def column(row, count):
    r = lax.broadcasted_iota(jnp.int32, (count, count), 0)
    c = lax.broadcasted_iota(jnp.int32, (count, count), 1)
    return jnp.sum(jnp.where(r == c, row, 0.0), axis=1, keepdims=True)


def stacked(v):
    hi, mid, lo = split3(v)
    return jnp.concatenate([hi, mid, lo, jnp.zeros_like(v)], axis=0).T.astype(BF16)


def kernel(
    nz, nh, width,
    dl_ref, x_ref, z_ref, b_ref, c_ref, step_ref, decay_ref, skip_ref, norm_ref, q_ref, k_ref, v_ref,
    so_ref, ao_ref,
    kv, s_in, s_out, local, pre, spread, e_parts, g_parts, row_parts, m_ref, bm_ref, cm_ref, rows_ref, bias_ref,
    kv_recv, z_send, x_send, s_recv, s_send,
):
    z = lax.axis_index("seq")
    x = lax.axis_index("head")
    rows, cols = x_ref.shape
    heads = step_ref.shape[0]
    nt = rows // TILE
    chunks = cols // width
    tok = q_ref.shape[0]
    kvw = k_ref.shape[1]
    slots = REACH * nh + 1
    own = slots - 1
    docs = dl_ref.shape[0]
    position = z * nh + x
    first = z * rows

    barrier = pltpu.get_barrier_semaphore()
    has_prev, has_next = z > 0, z < nz - 1

    def greet(axis, index):
        pl.semaphore_signal(barrier, inc=1, device_id={axis: index}, device_id_type=MESH)

    kv[own, :, :kvw] = k_ref[...]
    kv[own, :, kvw:] = v_ref[...]

    @pl.when(has_prev)
    def _():
        greet("seq", z - 1)

    @pl.when(has_next)
    def _():
        greet("seq", z + 1)

    for d in range(1, nh):
        greet("head", lax.rem(x + d, nh))

    pl.semaphore_wait(barrier, has_prev.astype(jnp.int32) + has_next.astype(jnp.int32) + nh - 1)

    def to_next(source, target, sem):
        return pltpu.make_async_remote_copy(
            src_ref=kv.at[source], dst_ref=kv.at[target], send_sem=z_send.at[sem], recv_sem=kv_recv.at[target],
            device_id={"seq": z + 1}, device_id_type=MESH)

    def to_side(source, target, sem, peer):
        return pltpu.make_async_remote_copy(
            src_ref=kv.at[source], dst_ref=kv.at[target], send_sem=x_send.at[sem], recv_sem=kv_recv.at[target],
            device_id={"head": peer}, device_id_type=MESH)

    def side_copies(d):
        up, down = x + d < nh, x - d >= 0
        base = (d - 1) * 4
        return {
            0: [(up, lambda: to_side(own, own - d, base, x + d))],
            1: [
                (up & has_prev, lambda: to_side(nh, nh - d, base + 1, x + d)),
                (down & has_prev, lambda: to_side(nh, nh + d, base + 2, x - d)),
            ],
            2: [(down & (z > 1), lambda: to_side(0, d, base + 3, x - d))],
        }

    def start_stage(stage):
        for d in range(1, nh):
            for exists, make in side_copies(d)[stage]:
                pl.when(exists)(lambda make=make: make().start())

    def arrived(slot):
        pltpu.make_async_copy(kv.at[slot], kv.at[slot], kv_recv.at[slot]).wait()

    pl.when(has_next)(lambda: to_next(own, nh, 0).start())
    start_stage(0)

    for slot in range(own):
        @pl.when(position - own + slot < 0)
        def _():
            kv[slot] = jnp.zeros((tok, 2 * kvw), BF16)

    @pl.when(z == 0)
    def _():
        s_in[...] = jnp.zeros_like(s_in)

    def doc_start(pos):
        best = jnp.zeros_like(pos)
        start = jnp.int32(0)
        for d in range(docs):
            best = jnp.where(start <= pos, jnp.maximum(best, start), best)
            start = start + dl_ref[d]
        return best

    end_start = doc_start(first + rows - 1)
    rates = column(-jnp.exp(decay_ref[...]), heads)
    step = step_ref[...]
    s_iota = lax.broadcasted_iota(jnp.int32, (rows, rows), 0)
    t_iota = lax.broadcasted_iota(jnp.int32, (rows, rows), 1)
    upper = jnp.where(s_iota <= t_iota, 1.0, 0.0).astype(BF16)
    hi, mid, lo = split3(step * rates)
    cum = dot(hi.astype(BF16), upper) + dot(mid.astype(BF16), upper) + dot(lo.astype(BF16), upper)
    last = cum[:, rows - 1 : rows]
    factor = jnp.where(end_start >= first, 0.0, jnp.exp(last))
    lane = lax.broadcasted_iota(jnp.int32, (heads, 128), 1)
    table = jnp.where(lane == 0, factor, jnp.where(lane == 1, column(skip_ref[...], heads), 0.0))
    pair = 0
    for i in range(nt):
        mark = i * TILE + TILE // 2 - 1
        ref = cum[:, mark : mark + 1]
        table = jnp.where(lane == 2 + 2 * i, jnp.exp(ref), table)
        table = jnp.where(lane == 3 + 2 * i, jnp.exp(last - ref), table)
        here = slice(i * TILE, (i + 1) * TILE)
        e_parts[here, :] = stacked(jnp.exp(cum[:, here] - ref))
        for j in range(i + 1):
            there = slice(j * TILE, (j + 1) * TILE)
            g_parts[pair] = stacked(jnp.exp(ref - cum[:, there]) * step[:, there])
            pair += 1
    row_parts[...] = stacked(table)[:16]
    r_iota = lax.broadcasted_iota(jnp.int32, spread.shape, 0)
    h_iota = lax.broadcasted_iota(jnp.int32, spread.shape, 1) // HEAD_P
    hit = r_iota == h_iota
    for piece in range(1, 4):
        hit = hit | (r_iota == h_iota + piece * heads)
    spread[...] = jnp.where(hit, 1.0, 0.0).astype(BF16)
    rows_ref[...] = dot(row_parts[...], spread[...])

    pos_t = first + lax.broadcasted_iota(jnp.int32, (rows, 1), 0)
    start_t = doc_start(pos_t)
    pos_s = first + lax.broadcasted_iota(jnp.int32, (rows, rows), 1)
    inter = dot_nt(c_ref[...], b_ref[...])
    m_ref[...] = jnp.where((pos_s >= start_t) & (pos_s <= pos_t), inter, 0.0).astype(BF16)
    bm_ref[...] = jnp.where(pos_t >= end_start, b_ref[...].astype(F32), 0.0).T.astype(BF16)
    cm_ref[...] = jnp.where(start_t < first, c_ref[...].astype(F32), 0.0).astype(BF16)
    query_t = position * tok + lax.broadcasted_iota(jnp.int32, (tok, 1), 0)
    key_s = (position - own) * tok + lax.broadcasted_iota(jnp.int32, (tok, slots * tok), 1)
    bias_ref[...] = jnp.where((key_s >= doc_start(query_t)) & (key_s <= query_t), 0.0, -jnp.inf)

    def state_copy(c):
        return pltpu.make_async_remote_copy(
            src_ref=s_out.at[c], dst_ref=s_in.at[c], send_sem=s_send.at[c], recv_sem=s_recv.at[c],
            device_id={"seq": z + 1}, device_id_type=MESH)

    def chunk_of(c):
        return pl.ds(pl.multiple_of(c * width, width), width)

    def block_part(c, _):
        at = chunk_of(c)
        state = jnp.zeros((bm_ref.shape[0], width), F32)
        pair = 0
        for i in range(nt):
            here = slice(i * TILE, (i + 1) * TILE)
            total = jnp.zeros((TILE, width), F32)
            for j in range(i + 1):
                there = slice(j * TILE, (j + 1) * TILE)
                scaled = (dot(g_parts[pair], spread[:, at]) * x_ref[there, at].astype(F32)).astype(BF16)
                total += dot(m_ref[here, there], scaled)
                pair += 1
            pre[here, at] = total
            state += dot(bm_ref[:, here], scaled) * rows_ref[3 + 2 * i : 4 + 2 * i, at]
        local[c] = state

        @pl.when(z == 0)
        def _():
            s_out[c] = state.astype(BF16)
            if nz > 1:
                state_copy(c).start()
        return 0

    lax.fori_loop(0, chunks, block_part, 0)

    @pl.when(has_prev)
    def _():
        arrived(nh)
        pl.when(has_next)(lambda: to_next(nh, 0, 1).start())

    start_stage(1)
    pl.when(z > 1)(lambda: arrived(0))
    start_stage(2)

    def state_part(c, squares):
        at = chunk_of(c)

        @pl.when(has_prev)
        def _():
            pltpu.make_async_copy(s_in.at[c], s_in.at[c], s_recv.at[c]).wait()

            @pl.when(has_next)
            def _():
                s_out[c] = (local[c] + rows_ref[0:1, at] * s_in[c].astype(F32)).astype(BF16)
                state_copy(c).start()

        inbound = s_in[c].astype(F32)
        sums = []
        for i in range(nt):
            here = slice(i * TILE, (i + 1) * TILE)
            scaled = (inbound * rows_ref[2 + 2 * i : 3 + 2 * i, at]).astype(BF16)
            total = (pre[here, at] + dot(cm_ref[here, :], scaled)) * dot(e_parts[here, :], spread[:, at])
            total += rows_ref[1:2, at] * x_ref[here, at].astype(F32)
            gate = z_ref[here, at].astype(F32)
            gated = total * (gate / (1.0 + jnp.exp(-gate)))
            pre[here, at] = gated
            sums.append(jnp.sum(gated * gated, axis=1, keepdims=True))
        return squares + jnp.concatenate(sums, axis=0)

    squares = lax.fori_loop(0, chunks, state_part, jnp.zeros((rows, 1), F32))
    inverse = lax.rsqrt(squares * (1.0 / cols) + 1e-05)

    def norm_part(c, _):
        at = chunk_of(c)
        so_ref[:, at] = (pre[:, at] * inverse * norm_ref[:, at]).astype(BF16)
        return 0

    lax.fori_loop(0, chunks, norm_part, 0)

    for slot in range(own):
        if slot not in (0, nh):
            pl.when(position - own + slot >= 0)(lambda slot=slot: arrived(slot))
    kv_heads = kvw // HEAD_D
    group = q_ref.shape[1] // kvw
    scale = 1.0 / math.sqrt(HEAD_D)

    def attend(g, _):
        def at(start):
            return pl.ds(pl.multiple_of(start, HEAD_D), HEAD_D)

        query = jnp.concatenate([q_ref[:, at((g * group + j) * HEAD_D)] for j in range(group)], axis=0)
        key = jnp.concatenate([kv[s, :, at(g * HEAD_D)] for s in range(slots)], axis=0)
        value = jnp.concatenate([kv[s, :, at(kvw + g * HEAD_D)] for s in range(slots)], axis=0)
        bias = jnp.concatenate([bias_ref[...]] * group, axis=0)
        logits = dot_nt(query, key) * scale + bias
        probs = jnp.exp(logits - jnp.max(logits, axis=1, keepdims=True))
        mixed = dot(probs.astype(BF16), value) / jnp.sum(probs, axis=1, keepdims=True)
        for j in range(group):
            ao_ref[:, at((g * group + j) * HEAD_D)] = mixed[j * tok : (j + 1) * tok].astype(BF16)
        return 0

    lax.fori_loop(0, kv_heads, attend, 0)

    @pl.when(has_next)
    def _():
        to_next(own, nh, 0).wait_send()
        pl.when(has_prev)(lambda: to_next(nh, 0, 1).wait_send())

        def sent(c, _):
            state_copy(c).wait_send()
            return 0

        lax.fori_loop(0, chunks, sent, 0)

    for d in range(1, nh):
        for copies in side_copies(d).values():
            for exists, make in copies:
                pl.when(exists)(lambda make=make: make().wait_send())


def on_device(
    nz, nh,
    ssm_input, ssm_gate, input_map, output_map, step_size, decay_log, skip_gain, norm_gain, doc_lengths,
    queries, keys_in, values_in,
):
    rows, cols = ssm_input.shape
    heads = step_size.shape[0]
    state = input_map.shape[1]
    tok, kvw = keys_in.shape
    width = min(512, cols)
    chunks = cols // width
    nt = rows // TILE
    slots = REACH * nh + 1
    vmem = pl.BlockSpec(memory_space=pltpu.VMEM)
    dma = pltpu.SemaphoreType.DMA
    return pl.pallas_call(
        functools.partial(kernel, nz, nh, width),
        out_shape=(
            jax.ShapeDtypeStruct((rows, cols), BF16),
            jax.ShapeDtypeStruct(queries.shape, BF16),
        ),
        in_specs=[pl.BlockSpec(memory_space=pltpu.SMEM)] + [vmem] * 11,
        out_specs=(vmem, vmem),
        scratch_shapes=[
            pltpu.VMEM((slots, tok, 2 * kvw), BF16),
            pltpu.VMEM((chunks, state, width), BF16),
            pltpu.VMEM((chunks, state, width), BF16),
            pltpu.VMEM((chunks, state, width), F32),
            pltpu.VMEM((rows, cols), F32),
            pltpu.VMEM((4 * heads, cols), BF16),
            pltpu.VMEM((rows, 4 * heads), BF16),
            pltpu.VMEM((nt * (nt + 1) // 2, TILE, 4 * heads), BF16),
            pltpu.VMEM((16, 4 * heads), BF16),
            pltpu.VMEM((rows, rows), BF16),
            pltpu.VMEM((state, rows), BF16),
            pltpu.VMEM((rows, state), BF16),
            pltpu.VMEM((16, cols), F32),
            pltpu.VMEM((tok, slots * tok), F32),
            dma((slots,)),
            dma((2,)),
            dma((max(1, 4 * (nh - 1)),)),
            dma((chunks,)),
            dma((chunks,)),
        ],
        compiler_params=pltpu.CompilerParams(
            collective_id=0, has_side_effects=True, vmem_limit_bytes=48 * 1024 * 1024
        ),
    )(
        doc_lengths, ssm_input, ssm_gate, input_map, output_map, step_size, decay_log[None, :], skip_gain[None, :],
        norm_gain[None, :], queries, keys_in, values_in,
    )


def solution(mesh):
    channels = P(("groups", "seq"), ("head", "tp"))
    per_head = P(("head", "tp"))
    positions = P(("groups", "seq", "head"), "tp")
    return jax.shard_map(
        functools.partial(on_device, mesh.shape["seq"], mesh.shape["head"]),
        mesh=mesh,
        in_specs=(
            channels, channels, channels, channels, P(("head", "tp"), ("groups", "seq")), per_head, per_head, per_head,
            P("groups"), positions, positions, positions,
        ),
        out_specs=(channels, positions),
        check_vma=False,
    )
```

time: 338 us -> 47 us (0.14)
  the two profiles are of different devices: /device:TPU:0 before, /device:TPU:24 now
where the time goes in v1:
time: 47 us; the launch traced here: 46.5 us
  Pallas kernels  35 us (74%)
  local copies, waits for them, and re-layouts  10.9 us (23%)
  between operations  0.68 us (1%)
    pallas_call x1, Pallas kernels, on_device(): pl.pallas_call(functools.partial(kernel, nz, nh, width), out_shape=(jax.S...  35 us
    unnamed x26, local copies, waits for them, and re-layouts  10.9 us

profile of v1, /device:TPU:24, one launch (start us, length us, event | category | flops | bytes accessed | tf_op | source)
XLA Modules:
  0.0 46.5 jit_solution(14217089849670873051)
XLA Ops:
  0.6 0.0 copy-start.9
  0.6 0.0 copy-start.10
  0.7 0.0 copy-start.11
  0.7 0.6 %copy-done.9 = s32[4]{0:T(128)S(1)} copy-done((s32[4]{0:T(128)S(1)}, s32[4]{0:T(128)}, u32[]{:S(2)}) %copy-start.9) | copy-done | bytes 40
  1.3 0.0 copy-done.10
  1.3 0.0 copy-done.11
  1.3 0.0 copy-start
  1.3 1.2 %copy-done = bf16[256,2048]{1,0:T(8,128)(2,1)S(1)} copy-done((bf16[256,2048]{1,0:T(8,128)(2,1)S(1)}, bf16[256,2048]{1,0:T(8,128)(2,1)}, u32[]{:S(2)}) %copy-start) | copy-done | bytes 1048600
  2.5 0.0 copy-start.1
  2.5 1.2 %copy-done.1 = bf16[256,2048]{1,0:T(8,128)(2,1)S(1)} copy-done((bf16[256,2048]{1,0:T(8,128)(2,1)S(1)}, bf16[256,2048]{1,0:T(8,128)(2,1)}, u32[]{:S(2)}) %copy-start.1) | copy-done | bytes 1048600
  3.8 0.0 copy-start.2
  3.8 1.0 %copy-done.2 = bf16[128,2048]{1,0:T(8,128)(2,1)S(1)} copy-done((bf16[128,2048]{1,0:T(8,128)(2,1)S(1)}, bf16[128,2048]{1,0:T(8,128)(2,1)}, u32[]{:S(2)}) %copy-start.2) | copy-done | bytes 524312
  4.8 0.0 copy-start.3
  4.8 0.9 %copy-done.3 = bf16[128,512]{1,0:T(8,128)(2,1)S(1)} copy-done((bf16[128,512]{1,0:T(8,128)(2,1)S(1)}, bf16[128,512]{1,0:T(8,128)(2,1)}, u32[]{:S(2)}) %copy-start.3) | copy-done | bytes 131096
  5.7 0.0 copy-start.4
  5.7 0.9 %copy-done.4 = bf16[128,512]{1,0:T(8,128)(2,1)S(1)} copy-done((bf16[128,512]{1,0:T(8,128)(2,1)S(1)}, bf16[128,512]{1,0:T(8,128)(2,1)}, u32[]{:S(2)}) %copy-start.4) | copy-done | bytes 131096
  6.6 0.0 copy-start.5
  6.6 0.8 %copy-done.5 = bf16[256,128]{1,0:T(8,128)(2,1)S(1)} copy-done((bf16[256,128]{1,0:T(8,128)(2,1)S(1)}, bf16[256,128]{1,0:T(8,128)(2,1)}, u32[]{:S(2)}) %copy-start.5) | copy-done | bytes 65560
  7.5 0.0 copy-start.6
  7.5 0.8 %copy-done.6 = bf16[256,128]{1,0:T(8,128)(2,1)S(1)} copy-done((bf16[256,128]{1,0:T(8,128)(2,1)S(1)}, bf16[256,128]{1,0:T(8,128)(2,1)}, u32[]{:S(2)}) %copy-start.6) | copy-done | bytes 65560
  8.3 0.0 copy-start.7
  8.3 0.8 %copy-done.7 = f32[32,256]{1,0:T(8,128)S(1)} copy-done((f32[32,256]{1,0:T(8,128)S(1)}, f32[32,256]{1,0:T(8,128)}, u32[]{:S(2)}) %copy-start.7) | copy-done | bytes 32792
  9.1 0.0 copy-start.8
  9.1 0.7 %copy-done.8 = f32[2048]{0:T(1024)S(1)} copy-done((f32[2048]{0:T(1024)S(1)}, f32[2048]{0:T(1024)}, u32[]{:S(2)}) %copy-start.8) | copy-done | bytes 8216
  9.8 35.0 %shard_map.131 = (bf16[256,2048]{1,0:T(8,128)(2,1)S(1)}, bf16[128,2048]{1,0:T(8,128)(2,1)S(1)}) custom-call(s32[4]{0:T(128)S(1)} %copy-done.9, bf16[256,2048]{1,0:T(8,128)(2,1)S(1)} %copy-done, bf16[256,2048]{1,0:T(8,128)(2,1)S(1)} %copy-done.1, bf16[256,128]{1,0:T(8,128)(2,1)S(1)} %copy-done.5, bf16[256,128]{1,0:T(8,128)(2,1)S(1)} %copy-done.6, ...), custom_call_target="tpu_custom_call" | custom-call | tf_op jit(solution)/shard_map/pallas_call | solution.py:316
  44.7 1.0 %copy.16 = bf16[256,2048]{1,0:T(8,128)(2,1)} copy(bf16[256,2048]{1,0:T(8,128)(2,1)S(1)} %get-tuple-element.4) | data formatting | bytes 2097152
  45.7 0.8 %copy.17 = bf16[128,2048]{1,0:T(8,128)(2,1)} copy(bf16[128,2048]{1,0:T(8,128)(2,1)S(1)} %get-tuple-element.5) | data formatting | bytes 1048576
Async XLA Ops:
  0.6 0.7 %copy-start.9 = (s32[4]{0:T(128)S(1)}, s32[4]{0:T(128)}, u32[]{:S(2)}) copy-start(s32[4]{0:T(128)} %dl_ref.1) | copy-start | bytes 52
  0.6 0.7 %copy-start.10 = (f32[32]{0:T(128)S(1)}, f32[32]{0:T(128)}, u32[]{:S(2)}) copy-start(f32[32]{0:T(128)} %param.17) | copy-start | bytes 388
  0.7 0.7 %copy-start.11 = (f32[32]{0:T(128)S(1)}, f32[32]{0:T(128)}, u32[]{:S(2)}) copy-start(f32[32]{0:T(128)} %param.18) | copy-start | bytes 388
  1.3 1.2 %copy-start = (bf16[256,2048]{1,0:T(8,128)(2,1)S(1)}, bf16[256,2048]{1,0:T(8,128)(2,1)}, u32[]{:S(2)}) copy-start(bf16[256,2048]{1,0:T(8,128)(2,1)} %x_ref.1) | copy-start | bytes 3145732
  2.5 1.2 %copy-start.1 = (bf16[256,2048]{1,0:T(8,128)(2,1)S(1)}, bf16[256,2048]{1,0:T(8,128)(2,1)}, u32[]{:S(2)}) copy-start(bf16[256,2048]{1,0:T(8,128)(2,1)} %z_ref.1) | copy-start | bytes 3145732
  3.8 1.0 %copy-start.2 = (bf16[128,2048]{1,0:T(8,128)(2,1)S(1)}, bf16[128,2048]{1,0:T(8,128)(2,1)}, u32[]{:S(2)}) copy-start(bf16[128,2048]{1,0:T(8,128)(2,1)} %q_ref.1) | copy-start | bytes 1572868
  4.8 0.9 %copy-start.3 = (bf16[128,512]{1,0:T(8,128)(2,1)S(1)}, bf16[128,512]{1,0:T(8,128)(2,1)}, u32[]{:S(2)}) copy-start(bf16[128,512]{1,0:T(8,128)(2,1)} %k_ref.1) | copy-start | bytes 393220
  5.7 0.9 %copy-start.4 = (bf16[128,512]{1,0:T(8,128)(2,1)S(1)}, bf16[128,512]{1,0:T(8,128)(2,1)}, u32[]{:S(2)}) copy-start(bf16[128,512]{1,0:T(8,128)(2,1)} %v_ref.1) | copy-start | bytes 393220
  6.6 0.8 %copy-start.5 = (bf16[256,128]{1,0:T(8,128)(2,1)S(1)}, bf16[256,128]{1,0:T(8,128)(2,1)}, u32[]{:S(2)}) copy-start(bf16[256,128]{1,0:T(8,128)(2,1)} %b_ref.1) | copy-start | bytes 196612
  7.5 0.8 %copy-start.6 = (bf16[256,128]{1,0:T(8,128)(2,1)S(1)}, bf16[256,128]{1,0:T(8,128)(2,1)}, u32[]{:S(2)}) copy-start(bf16[256,128]{1,0:T(8,128)(2,1)} %c_ref.1) | copy-start | bytes 196612
  8.3 0.8 %copy-start.7 = (f32[32,256]{1,0:T(8,128)S(1)}, f32[32,256]{1,0:T(8,128)}, u32[]{:S(2)}) copy-start(f32[32,256]{1,0:T(8,128)} %step_ref.1) | copy-start | bytes 98308
  9.1 0.7 %copy-start.8 = (f32[2048]{0:T(1024)S(1)}, f32[2048]{0:T(1024)}, u32[]{:S(2)}) copy-start(f32[2048]{0:T(1024)} %param.19) | copy-start | bytes 24580

commit v2 on v1

--- a/solution.py
+++ b/solution.py
@@ -45,10 +45,12 @@
 
 def kernel(
     nz, nh, width,
-    dl_ref, x_ref, z_ref, b_ref, c_ref, step_ref, decay_ref, skip_ref, norm_ref, q_ref, k_ref, v_ref,
+    dl_hbm, x_hbm, z_hbm, b_hbm, c_hbm, step_hbm, decay_hbm, skip_hbm, norm_hbm, q_hbm, k_hbm, v_hbm,
     so_ref, ao_ref,
+    dl_ref, x_ref, z_ref, b_ref, c_ref, step_ref, decay_ref, skip_ref, norm_ref, q_ref,
     kv, s_in, s_out, local, pre, spread, e_parts, g_parts, row_parts, m_ref, bm_ref, cm_ref, rows_ref, bias_ref,
-    kv_recv, z_send, x_send, s_recv, s_send,
+    mixed_ref, top_ref, sum_ref,
+    loads, kv_recv, z_send, x_send, s_recv, s_send,
 ):
     z = lax.axis_index("seq")
     x = lax.axis_index("head")
@@ -57,7 +59,7 @@
     nt = rows // TILE
     chunks = cols // width
     tok = q_ref.shape[0]
-    kvw = k_ref.shape[1]
+    kvw = k_hbm.shape[1]
     slots = REACH * nh + 1
     own = slots - 1
     docs = dl_ref.shape[0]
@@ -70,8 +72,14 @@
     def greet(axis, index):
         pl.semaphore_signal(barrier, inc=1, device_id={axis: index}, device_id_type=MESH)
 
-    kv[own, :, :kvw] = k_ref[...]
-    kv[own, :, kvw:] = v_ref[...]
+    moves = [
+        (k_hbm, kv.at[own, :, pl.ds(0, kvw)]), (v_hbm, kv.at[own, :, pl.ds(kvw, kvw)]), (step_hbm, step_ref),
+        (decay_hbm, decay_ref), (skip_hbm, skip_ref), (dl_hbm, dl_ref), (b_hbm, b_ref), (c_hbm, c_ref), (x_hbm, x_ref),
+        (q_hbm, q_ref), (z_hbm, z_ref), (norm_hbm, norm_ref),
+    ]
+    moves = [pltpu.make_async_copy(source, target, loads.at[i]) for i, (source, target) in enumerate(moves)]
+    for move in moves:
+        move.start()
 
     @pl.when(has_prev)
     def _():
@@ -85,6 +93,9 @@
         greet("head", lax.rem(x + d, nh))
 
     pl.semaphore_wait(barrier, has_prev.astype(jnp.int32) + has_next.astype(jnp.int32) + nh - 1)
+
+    moves[0].wait()
+    moves[1].wait()
 
     def to_next(source, target, sem):
         return pltpu.make_async_remote_copy(
@@ -127,6 +138,9 @@
     @pl.when(z == 0)
     def _():
         s_in[...] = jnp.zeros_like(s_in)
+
+    for move in moves[2:8]:
+        move.wait()
 
     def doc_start(pos):
         best = jnp.zeros_like(pos)
@@ -211,7 +225,10 @@
                 state_copy(c).start()
         return 0
 
+    moves[8].wait()
     lax.fori_loop(0, chunks, block_part, 0)
+    for move in moves[9:]:
+        move.wait()
 
     @pl.when(has_prev)
     def _():
@@ -219,8 +236,44 @@
         pl.when(has_next)(lambda: to_next(nh, 0, 1).start())
 
     start_stage(1)
-    pl.when(z > 1)(lambda: arrived(0))
-    start_stage(2)
+    kv_heads = kvw // HEAD_D
+    group = q_hbm.shape[1] // kvw
+    scale = 1.0 / math.sqrt(HEAD_D)
+
+    def head_at(start):
+        return pl.ds(pl.multiple_of(start, HEAD_D), HEAD_D)
+
+    def logits_of(g, low, high):
+        query = jnp.concatenate([q_ref[:, head_at((g * group + j) * HEAD_D)] for j in range(group)], axis=0)
+        key = jnp.concatenate([kv[s, :, head_at(g * HEAD_D)] for s in range(low, high)], axis=0)
+        value = jnp.concatenate([kv[s, :, head_at(kvw + g * HEAD_D)] for s in range(low, high)], axis=0)
+        bias = jnp.concatenate([bias_ref[:, low * tok : high * tok]] * group, axis=0)
+        return dot_nt(query, key) * scale + bias, value
+
+    def near(g):
+        logits, value = logits_of(g, nh, slots)
+        top = jnp.max(logits, axis=1, keepdims=True)
+        probs = jnp.exp(logits - top)
+        mixed_ref[g] = dot(probs.astype(BF16), value)
+        top_ref[g] = top
+        sum_ref[g] = jnp.sum(probs, axis=1, keepdims=True)
+
+    def far(g, _):
+        logits, value = logits_of(g, 0, nh)
+        before = top_ref[g]
+        top = jnp.maximum(before, jnp.max(logits, axis=1, keepdims=True))
+        probs = jnp.exp(logits - top)
+        keep = jnp.exp(before - top)
+        total = jnp.sum(probs, axis=1, keepdims=True) + sum_ref[g] * keep
+        mixed = (dot(probs.astype(BF16), value) + mixed_ref[g] * keep) / total
+        for j in range(group):
+            ao_ref[:, head_at((g * group + j) * HEAD_D)] = mixed[j * tok : (j + 1) * tok].astype(BF16)
+        return 0
+
+    def far_all():
+        for slot in range(1, nh):
+            pl.when(position - own + slot >= 0)(lambda slot=slot: arrived(slot))
+        lax.fori_loop(0, kv_heads, far, 0)
 
     def state_part(c, squares):
         at = chunk_of(c)
@@ -247,7 +300,28 @@
             sums.append(jnp.sum(gated * gated, axis=1, keepdims=True))
         return squares + jnp.concatenate(sums, axis=0)
 
-    squares = lax.fori_loop(0, chunks, state_part, jnp.zeros((rows, 1), F32))
+    def near_part(g, _):
+        near(g)
+        return 0
+
+    def mixed_part(c, squares):
+        squares = state_part(c, squares)
+
+        @pl.when(c == 0)
+        def _():
+            for slot in range(nh + 1, own):
+                pl.when(position - own + slot >= 0)(lambda slot=slot: arrived(slot))
+
+        pl.when(c < kv_heads)(lambda: near(c))
+        return squares
+
+    squares = mixed_part(0, jnp.zeros((rows, 1), F32))
+    pl.when(z > 1)(lambda: arrived(0))
+    start_stage(2)
+    squares = lax.fori_loop(1, chunks - 1, mixed_part, squares)
+    lax.fori_loop(chunks - 1, kv_heads, near_part, 0)
+    pl.when(z == nz - 1)(far_all)
+    squares = state_part(chunks - 1, squares)
     inverse = lax.rsqrt(squares * (1.0 / cols) + 1e-05)
 
     def norm_part(c, _):
@@ -256,30 +330,7 @@
         return 0
 
     lax.fori_loop(0, chunks, norm_part, 0)
-
-    for slot in range(own):
-        if slot not in (0, nh):
-            pl.when(position - own + slot >= 0)(lambda slot=slot: arrived(slot))
-    kv_heads = kvw // HEAD_D
-    group = q_ref.shape[1] // kvw
-    scale = 1.0 / math.sqrt(HEAD_D)
-
-    def attend(g, _):
-        def at(start):
-            return pl.ds(pl.multiple_of(start, HEAD_D), HEAD_D)
-
-        query = jnp.concatenate([q_ref[:, at((g * group + j) * HEAD_D)] for j in range(group)], axis=0)
-        key = jnp.concatenate([kv[s, :, at(g * HEAD_D)] for s in range(slots)], axis=0)
-        value = jnp.concatenate([kv[s, :, at(kvw + g * HEAD_D)] for s in range(slots)], axis=0)
-        bias = jnp.concatenate([bias_ref[...]] * group, axis=0)
-        logits = dot_nt(query, key) * scale + bias
-        probs = jnp.exp(logits - jnp.max(logits, axis=1, keepdims=True))
-        mixed = dot(probs.astype(BF16), value) / jnp.sum(probs, axis=1, keepdims=True)
-        for j in range(group):
-            ao_ref[:, at((g * group + j) * HEAD_D)] = mixed[j * tok : (j + 1) * tok].astype(BF16)
-        return 0
-
-    lax.fori_loop(0, kv_heads, attend, 0)
+    pl.when(z < nz - 1)(far_all)
 
     @pl.when(has_next)
     def _():
@@ -319,9 +370,19 @@
             jax.ShapeDtypeStruct((rows, cols), BF16),
             jax.ShapeDtypeStruct(queries.shape, BF16),
         ),
-        in_specs=[pl.BlockSpec(memory_space=pltpu.SMEM)] + [vmem] * 11,
+        in_specs=[pl.BlockSpec(memory_space=pltpu.HBM)] * 12,
         out_specs=(vmem, vmem),
         scratch_shapes=[
+            pltpu.SMEM(doc_lengths.shape, jnp.int32),
+            pltpu.VMEM((rows, cols), BF16),
+            pltpu.VMEM((rows, cols), BF16),
+            pltpu.VMEM((rows, state), BF16),
+            pltpu.VMEM((rows, state), BF16),
+            pltpu.VMEM((heads, rows), F32),
+            pltpu.VMEM((1, heads), F32),
+            pltpu.VMEM((1, heads), F32),
+            pltpu.VMEM((1, cols), F32),
+            pltpu.VMEM(queries.shape, BF16),
             pltpu.VMEM((slots, tok, 2 * kvw), BF16),
             pltpu.VMEM((chunks, state, width), BF16),
             pltpu.VMEM((chunks, state, width), BF16),
@@ -336,6 +397,10 @@
             pltpu.VMEM((rows, state), BF16),
             pltpu.VMEM((16, cols), F32),
             pltpu.VMEM((tok, slots * tok), F32),
+            pltpu.VMEM((kvw // HEAD_D, tok * queries.shape[1] // kvw, HEAD_D), F32),
+            pltpu.VMEM((kvw // HEAD_D, tok * queries.shape[1] // kvw, 1), F32),
+            pltpu.VMEM((kvw // HEAD_D, tok * queries.shape[1] // kvw, 1), F32),
+            dma((12,)),
             dma((slots,)),
             dma((2,)),
             dma((max(1, 4 * (nh - 1)),)),
@@ -343,7 +408,7 @@
             dma((chunks,)),
         ],
         compiler_params=pltpu.CompilerParams(
-            collective_id=0, has_side_effects=True, vmem_limit_bytes=48 * 1024 * 1024
+            collective_id=0, has_side_effects=True, vmem_limit_bytes=60 * 1024 * 1024
         ),
     )(
         doc_lengths, ssm_input, ssm_gate, input_map, output_map, step_size, decay_log[None, :], skip_gain[None, :],

time: 47 us -> 43.7 us (0.930)
  local copies, waits for them, and re-layouts: 10.9 us -> 3.16 us
  Pallas kernels: 35 us -> 39.8 us
    unnamed x26 -> x4, local copies, waits for them, and re-layouts: 10.9 us -> 3.16 us
    pallas_call x1, Pallas kernels: 35 us -> 39.8 us  [on_device(): pl.pallas_call(functools.partial(kernel, nz, nh, width), out_shape=(jax.S...]
where the time goes in v2:
time: 43.7 us; the launch traced here: 43.6 us
  Pallas kernels  39.8 us (91%)
  local copies, waits for them, and re-layouts  3.16 us (7%)
  between operations  0.65 us (1%)
    pallas_call x1, Pallas kernels, on_device(): pl.pallas_call(functools.partial(kernel, nz, nh, width), out_shape=(jax.S...  39.8 us
    unnamed x4, local copies, waits for them, and re-layouts  3.16 us

profile of v2, /device:TPU:24, one launch (start us, length us, event | category | flops | bytes accessed | tf_op | source)
XLA Modules:
  0.0 43.6 jit_solution(8670517906445409401)
XLA Ops:
  0.6 39.8 %shard_map.131 = (bf16[256,2048]{1,0:T(8,128)(2,1)}, bf16[128,2048]{1,0:T(8,128)(2,1)}) custom-call(s32[4]{0:T(128)} %dl_hbm.1, bf16[256,2048]{1,0:T(8,128)(2,1)} %x_hbm.1, bf16[256,2048]{1,0:T(8,128)(2,1)} %z_hbm.1, bf16[256,128]{1,0:T(8,128)(2,1)} %b_hbm.1, bf16[256,128]{1,0:T(8,128)(2,1)} %c_hbm.1, f32[32,256]{1,0:T(8,128)} %step_hbm.1, f32[1,32]{1,0:T(1,128)} %bitcast.4, ...), custom_call_target="tpu_custom_call" | custom-call | tf_op jit(solution)/shard_map/pallas_call | solution.py:367
  40.4 0.0 copy-start
  40.4 2.4 %copy.16 = bf16[256,2048]{1,0:T(8,128)(2,1)} copy(bf16[256,2048]{1,0:T(8,128)(2,1)} %get-tuple-element.4) | data formatting | bytes 2097152
  42.8 0.0 copy-done
  42.8 0.8 %copy.17 = bf16[128,2048]{1,0:T(8,128)(2,1)} copy(bf16[128,2048]{1,0:T(8,128)(2,1)S(1)} %copy-done) | data formatting | bytes 1048576
Async XLA Ops:
  40.4 2.4 %copy-start = (bf16[128,2048]{1,0:T(8,128)(2,1)S(1)}, bf16[128,2048]{1,0:T(8,128)(2,1)}, u32[]{:S(2)}) copy-start(bf16[128,2048]{1,0:T(8,128)(2,1)} %get-tuple-element.5) | copy-start | bytes 1572868

commit v3 on v2

--- a/solution.py
+++ b/solution.py
@@ -72,8 +72,15 @@
     def greet(axis, index):
         pl.semaphore_signal(barrier, inc=1, device_id={axis: index}, device_id_type=MESH)
 
-    moves = [
-        (k_hbm, kv.at[own, :, pl.ds(0, kvw)]), (v_hbm, kv.at[own, :, pl.ds(kvw, kvw)]), (step_hbm, step_ref),
+    kv_heads = kvw // HEAD_D
+    moves = []
+    for g in range(kv_heads):
+        for i, source in enumerate((k_hbm, v_hbm)):
+            moves.append((
+                source.at[:, pl.ds(g * HEAD_D, HEAD_D)], kv.at[own, g, :, pl.ds(i * HEAD_D, HEAD_D)]))
+    early = len(moves)
+    moves += [
+        (step_hbm, step_ref),
         (decay_hbm, decay_ref), (skip_hbm, skip_ref), (dl_hbm, dl_ref), (b_hbm, b_ref), (c_hbm, c_ref), (x_hbm, x_ref),
         (q_hbm, q_ref), (z_hbm, z_ref), (norm_hbm, norm_ref),
     ]
@@ -94,52 +101,56 @@
 
     pl.semaphore_wait(barrier, has_prev.astype(jnp.int32) + has_next.astype(jnp.int32) + nh - 1)
 
-    moves[0].wait()
-    moves[1].wait()
-
-    def to_next(source, target, sem):
+    for move in moves[:early]:
+        move.wait()
+
+    def to_next(source, target, sem, g):
         return pltpu.make_async_remote_copy(
-            src_ref=kv.at[source], dst_ref=kv.at[target], send_sem=z_send.at[sem], recv_sem=kv_recv.at[target],
-            device_id={"seq": z + 1}, device_id_type=MESH)
-
-    def to_side(source, target, sem, peer):
+            src_ref=kv.at[source, g], dst_ref=kv.at[target, g], send_sem=z_send.at[sem, g],
+            recv_sem=kv_recv.at[target, g], device_id={"seq": z + 1}, device_id_type=MESH)
+
+    def to_side(source, target, sem, peer, g):
         return pltpu.make_async_remote_copy(
-            src_ref=kv.at[source], dst_ref=kv.at[target], send_sem=x_send.at[sem], recv_sem=kv_recv.at[target],
-            device_id={"head": peer}, device_id_type=MESH)
-
-    def side_copies(d):
+            src_ref=kv.at[source, g], dst_ref=kv.at[target, g], send_sem=x_send.at[sem, g],
+            recv_sem=kv_recv.at[target, g], device_id={"head": peer}, device_id_type=MESH)
+
+    def side_copies(d, g):
         up, down = x + d < nh, x - d >= 0
         base = (d - 1) * 4
         return {
-            0: [(up, lambda: to_side(own, own - d, base, x + d))],
+            0: [(up, lambda: to_side(own, own - d, base, x + d, g))],
             1: [
-                (up & has_prev, lambda: to_side(nh, nh - d, base + 1, x + d)),
-                (down & has_prev, lambda: to_side(nh, nh + d, base + 2, x - d)),
+                (up & has_prev, lambda: to_side(nh, nh - d, base + 1, x + d, g)),
+                (down & has_prev, lambda: to_side(nh, nh + d, base + 2, x - d, g)),
             ],
-            2: [(down & (z > 1), lambda: to_side(0, d, base + 3, x - d))],
+            2: [(down & (z > 1), lambda: to_side(0, d, base + 3, x - d, g))],
         }
 
-    def start_stage(stage):
+    def start_stage(stage, g):
         for d in range(1, nh):
-            for exists, make in side_copies(d)[stage]:
+            for exists, make in side_copies(d, g)[stage]:
                 pl.when(exists)(lambda make=make: make().start())
 
-    def arrived(slot):
-        pltpu.make_async_copy(kv.at[slot], kv.at[slot], kv_recv.at[slot]).wait()
-
-    pl.when(has_next)(lambda: to_next(own, nh, 0).start())
-    start_stage(0)
+    def arrived(slot, g):
+        pltpu.make_async_copy(kv.at[slot, g], kv.at[slot, g], kv_recv.at[slot, g]).wait()
+
+    def send_own(g, _):
+        pl.when(has_next)(lambda: to_next(own, nh, 0, g).start())
+        start_stage(0, g)
+        return 0
+
+    lax.fori_loop(0, kv_heads, send_own, 0)
 
     for slot in range(own):
         @pl.when(position - own + slot < 0)
         def _():
-            kv[slot] = jnp.zeros((tok, 2 * kvw), BF16)
+            kv[slot] = jnp.zeros(kv.shape[1:], BF16)
 
     @pl.when(z == 0)
     def _():
         s_in[...] = jnp.zeros_like(s_in)
 
-    for move in moves[2:8]:
+    for move in moves[early : early + 6]:
         move.wait()
 
     def doc_start(pos):
@@ -225,18 +236,22 @@
                 state_copy(c).start()
         return 0
 
-    moves[8].wait()
+    moves[early + 6].wait()
     lax.fori_loop(0, chunks, block_part, 0)
-    for move in moves[9:]:
+    for move in moves[early + 7 :]:
         move.wait()
 
-    @pl.when(has_prev)
-    def _():
-        arrived(nh)
-        pl.when(has_next)(lambda: to_next(nh, 0, 1).start())
-
-    start_stage(1)
-    kv_heads = kvw // HEAD_D
+    def relay(g, _):
+        @pl.when(has_prev)
+        def _():
+            arrived(nh, g)
+            pl.when(has_next)(lambda: to_next(nh, 0, 1, g).start())
+
+        start_stage(1, g)
+        return 0
+
+    lax.fori_loop(0, kv_heads, relay, 0)
+
     group = q_hbm.shape[1] // kvw
     scale = 1.0 / math.sqrt(HEAD_D)
 
@@ -245,12 +260,14 @@
 
     def logits_of(g, low, high):
         query = jnp.concatenate([q_ref[:, head_at((g * group + j) * HEAD_D)] for j in range(group)], axis=0)
-        key = jnp.concatenate([kv[s, :, head_at(g * HEAD_D)] for s in range(low, high)], axis=0)
-        value = jnp.concatenate([kv[s, :, head_at(kvw + g * HEAD_D)] for s in range(low, high)], axis=0)
+        key = jnp.concatenate([kv[s, g, :, :HEAD_D] for s in range(low, high)], axis=0)
+        value = jnp.concatenate([kv[s, g, :, HEAD_D:] for s in range(low, high)], axis=0)
         bias = jnp.concatenate([bias_ref[:, low * tok : high * tok]] * group, axis=0)
         return dot_nt(query, key) * scale + bias, value
 
     def near(g):
+        for slot in range(nh + 1, own):
+            pl.when(position - own + slot >= 0)(lambda slot=slot: arrived(slot, g))
         logits, value = logits_of(g, nh, slots)
         top = jnp.max(logits, axis=1, keepdims=True)
         probs = jnp.exp(logits - top)
@@ -258,7 +275,9 @@
         top_ref[g] = top
         sum_ref[g] = jnp.sum(probs, axis=1, keepdims=True)
 
-    def far(g, _):
+    def far(g):
+        for slot in range(1, nh):
+            pl.when(position - own + slot >= 0)(lambda slot=slot: arrived(slot, g))
         logits, value = logits_of(g, 0, nh)
         before = top_ref[g]
         top = jnp.maximum(before, jnp.max(logits, axis=1, keepdims=True))
@@ -268,12 +287,6 @@
         mixed = (dot(probs.astype(BF16), value) + mixed_ref[g] * keep) / total
         for j in range(group):
             ao_ref[:, head_at((g * group + j) * HEAD_D)] = mixed[j * tok : (j + 1) * tok].astype(BF16)
-        return 0
-
-    def far_all():
-        for slot in range(1, nh):
-            pl.when(position - own + slot >= 0)(lambda slot=slot: arrived(slot))
-        lax.fori_loop(0, kv_heads, far, 0)
 
     def state_part(c, squares):
         at = chunk_of(c)
@@ -300,28 +313,20 @@
             sums.append(jnp.sum(gated * gated, axis=1, keepdims=True))
         return squares + jnp.concatenate(sums, axis=0)
 
-    def near_part(g, _):
-        near(g)
-        return 0
-
-    def mixed_part(c, squares):
+    def far_start(g):
+        pl.when(z > 1)(lambda: arrived(0, g))
+        start_stage(2, g)
+
+    def step_part(c, squares):
+        near_g, start_g, far_g = c, c, c - (chunks - kv_heads)
+        pl.when((far_g >= 0) & (far_g < kv_heads) )(lambda: far(far_g))
+        pl.when((start_g >= 0) & (start_g < kv_heads))(lambda: far_start(start_g))
         squares = state_part(c, squares)
-
-        @pl.when(c == 0)
-        def _():
-            for slot in range(nh + 1, own):
-                pl.when(position - own + slot >= 0)(lambda slot=slot: arrived(slot))
-
-        pl.when(c < kv_heads)(lambda: near(c))
+        pl.when((near_g >= 0) & (near_g < kv_heads))(lambda: near(near_g))
         return squares
 
-    squares = mixed_part(0, jnp.zeros((rows, 1), F32))
-    pl.when(z > 1)(lambda: arrived(0))
-    start_stage(2)
-    squares = lax.fori_loop(1, chunks - 1, mixed_part, squares)
-    lax.fori_loop(chunks - 1, kv_heads, near_part, 0)
-    pl.when(z == nz - 1)(far_all)
-    squares = state_part(chunks - 1, squares)
+    at_end = z == nz - 1
+    squares = lax.fori_loop(0, chunks, step_part, jnp.zeros((rows, 1), F32))
     inverse = lax.rsqrt(squares * (1.0 / cols) + 1e-05)
 
     def norm_part(c, _):
@@ -330,12 +335,16 @@
         return 0
 
     lax.fori_loop(0, chunks, norm_part, 0)
-    pl.when(z < nz - 1)(far_all)
+
 
     @pl.when(has_next)
     def _():
-        to_next(own, nh, 0).wait_send()
-        pl.when(has_prev)(lambda: to_next(nh, 0, 1).wait_send())
+        def passed(g, _):
+            to_next(own, nh, 0, g).wait_send()
+            pl.when(has_prev)(lambda: to_next(nh, 0, 1, g).wait_send())
+            return 0
+
+        lax.fori_loop(0, kv_heads, passed, 0)
 
         def sent(c, _):
             state_copy(c).wait_send()
@@ -343,10 +352,14 @@
 
         lax.fori_loop(0, chunks, sent, 0)
 
-    for d in range(1, nh):
-        for copies in side_copies(d).values():
-            for exists, make in copies:
-                pl.when(exists)(lambda make=make: make().wait_send())
+    def side_passed(g, _):
+        for d in range(1, nh):
+            for copies in side_copies(d, g).values():
+                for exists, make in copies:
+                    pl.when(exists)(lambda make=make: make().wait_send())
+        return 0
+
+    lax.fori_loop(0, kv_heads, side_passed, 0)
 
 
 def on_device(
@@ -358,7 +371,7 @@
     heads = step_size.shape[0]
     state = input_map.shape[1]
     tok, kvw = keys_in.shape
-    width = min(512, cols)
+    width = cols // 8
     chunks = cols // width
     nt = rows // TILE
     slots = REACH * nh + 1
@@ -383,7 +396,7 @@
             pltpu.VMEM((1, heads), F32),
             pltpu.VMEM((1, cols), F32),
             pltpu.VMEM(queries.shape, BF16),
-            pltpu.VMEM((slots, tok, 2 * kvw), BF16),
+            pltpu.VMEM((slots, kvw // HEAD_D, tok, 2 * HEAD_D), BF16),
             pltpu.VMEM((chunks, state, width), BF16),
             pltpu.VMEM((chunks, state, width), BF16),
             pltpu.VMEM((chunks, state, width), F32),
@@ -400,10 +413,10 @@
             pltpu.VMEM((kvw // HEAD_D, tok * queries.shape[1] // kvw, HEAD_D), F32),
             pltpu.VMEM((kvw // HEAD_D, tok * queries.shape[1] // kvw, 1), F32),
             pltpu.VMEM((kvw // HEAD_D, tok * queries.shape[1] // kvw, 1), F32),
-            dma((12,)),
-            dma((slots,)),
-            dma((2,)),
-            dma((max(1, 4 * (nh - 1)),)),
+            dma((10 + 2 * (kvw // HEAD_D),)),
+            dma((slots, kvw // HEAD_D)),
+            dma((2, kvw // HEAD_D)),
+            dma((max(1, 4 * (nh - 1)), kvw // HEAD_D)),
             dma((chunks,)),
             dma((chunks,)),
         ],

time: 43.7 us -> 38.7 us (0.89)
  Pallas kernels: 39.8 us -> 34.7 us
    pallas_call x1, Pallas kernels: 39.8 us -> 34.7 us  [on_device(): pl.pallas_call(functools.partial(kernel, nz, nh, width), out_shape=(jax.S...]
where the time goes in v3:
time: 38.7 us; the launch traced here: 38.5 us
  Pallas kernels  34.7 us (90%)
  local copies, waits for them, and re-layouts  3.16 us (8%)
  between operations  0.65 us (2%)
    pallas_call x1, Pallas kernels, on_device(): pl.pallas_call(functools.partial(kernel, nz, nh, width), out_shape=(jax.S...  34.7 us
    unnamed x4, local copies, waits for them, and re-layouts  3.16 us

profile of v3, /device:TPU:24, one launch (start us, length us, event | category | flops | bytes accessed | tf_op | source)
XLA Modules:
  0.0 38.5 jit_solution(14199976364492593637)
XLA Ops:
  0.6 34.7 %shard_map.131 = (bf16[256,2048]{1,0:T(8,128)(2,1)}, bf16[128,2048]{1,0:T(8,128)(2,1)}) custom-call(s32[4]{0:T(128)} %dl_hbm.1, bf16[256,2048]{1,0:T(8,128)(2,1)} %x_hbm.1, bf16[256,2048]{1,0:T(8,128)(2,1)} %z_hbm.1, bf16[256,128]{1,0:T(8,128)(2,1)} %b_hbm.1, bf16[256,128]{1,0:T(8,128)(2,1)} %c_hbm.1, f32[32,256]{1,0:T(8,128)} %step_hbm.1, f32[1,32]{1,0:T(1,128)} %bitcast.4, ...), custom_call_target="tpu_custom_call" | custom-call | tf_op jit(solution)/shard_map/pallas_call | solution.py:380
  35.4 0.0 copy-start
  35.4 2.4 %copy.16 = bf16[256,2048]{1,0:T(8,128)(2,1)} copy(bf16[256,2048]{1,0:T(8,128)(2,1)} %get-tuple-element.4) | data formatting | bytes 2097152
  37.7 0.0 copy-done
  37.7 0.8 %copy.17 = bf16[128,2048]{1,0:T(8,128)(2,1)} copy(bf16[128,2048]{1,0:T(8,128)(2,1)S(1)} %copy-done) | data formatting | bytes 1048576
Async XLA Ops:
  35.4 2.4 %copy-start = (bf16[128,2048]{1,0:T(8,128)(2,1)S(1)}, bf16[128,2048]{1,0:T(8,128)(2,1)}, u32[]{:S(2)}) copy-start(bf16[128,2048]{1,0:T(8,128)(2,1)} %get-tuple-element.5) | copy-start | bytes 1572868

commit v4 on v3

--- a/solution.py
+++ b/solution.py
@@ -46,11 +46,11 @@
 def kernel(
     nz, nh, width,
     dl_hbm, x_hbm, z_hbm, b_hbm, c_hbm, step_hbm, decay_hbm, skip_hbm, norm_hbm, q_hbm, k_hbm, v_hbm,
-    so_ref, ao_ref,
-    dl_ref, x_ref, z_ref, b_ref, c_ref, step_ref, decay_ref, skip_ref, norm_ref, q_ref,
+    so_hbm, ao_hbm,
+    so_ref, ao_ref, dl_ref, x_ref, z_ref, b_ref, c_ref, step_ref, decay_ref, skip_ref, norm_ref, q_ref,
     kv, s_in, s_out, local, pre, spread, e_parts, g_parts, row_parts, m_ref, bm_ref, cm_ref, rows_ref, bias_ref,
     mixed_ref, top_ref, sum_ref,
-    loads, kv_recv, z_send, x_send, s_recv, s_send,
+    loads, so_done, ao_done, kv_recv, z_send, x_send, s_recv, s_send,
 ):
     z = lax.axis_index("seq")
     x = lax.axis_index("head")
@@ -265,6 +265,13 @@
         bias = jnp.concatenate([bias_ref[:, low * tok : high * tok]] * group, axis=0)
         return dot_nt(query, key) * scale + bias, value
 
+    def so_copy(c):
+        return pltpu.make_async_copy(so_ref.at[:, chunk_of(c)], so_hbm.at[:, chunk_of(c)], so_done.at[c])
+
+    def ao_copy(g):
+        at = pl.ds(pl.multiple_of(g * group * HEAD_D, HEAD_D), group * HEAD_D)
+        return pltpu.make_async_copy(ao_ref.at[:, at], ao_hbm.at[:, at], ao_done.at[g])
+
     def near(g):
         for slot in range(nh + 1, own):
             pl.when(position - own + slot >= 0)(lambda slot=slot: arrived(slot, g))
@@ -287,6 +294,7 @@
         mixed = (dot(probs.astype(BF16), value) + mixed_ref[g] * keep) / total
         for j in range(group):
             ao_ref[:, head_at((g * group + j) * HEAD_D)] = mixed[j * tok : (j + 1) * tok].astype(BF16)
+        ao_copy(g).start()
 
     def state_part(c, squares):
         at = chunk_of(c)
@@ -318,24 +326,41 @@
         start_stage(2, g)
 
     def step_part(c, squares):
-        near_g, start_g, far_g = c, c, c - (chunks - kv_heads)
+        near_g, far_g = c, c - (chunks - kv_heads)
         pl.when((far_g >= 0) & (far_g < kv_heads) )(lambda: far(far_g))
-        pl.when((start_g >= 0) & (start_g < kv_heads))(lambda: far_start(start_g))
         squares = state_part(c, squares)
         pl.when((near_g >= 0) & (near_g < kv_heads))(lambda: near(near_g))
         return squares
 
     at_end = z == nz - 1
+
+    def start_part(g, _):
+        far_start(g)
+        return 0
+
+    lax.fori_loop(0, kv_heads, start_part, 0)
     squares = lax.fori_loop(0, chunks, step_part, jnp.zeros((rows, 1), F32))
     inverse = lax.rsqrt(squares * (1.0 / cols) + 1e-05)
 
     def norm_part(c, _):
         at = chunk_of(c)
         so_ref[:, at] = (pre[:, at] * inverse * norm_ref[:, at]).astype(BF16)
+        so_copy(c).start()
         return 0
 
     lax.fori_loop(0, chunks, norm_part, 0)
 
+
+    def so_left(c, _):
+        so_copy(c).wait()
+        return 0
+
+    def ao_left(g, _):
+        ao_copy(g).wait()
+        return 0
+
+    lax.fori_loop(0, chunks, so_left, 0)
+    lax.fori_loop(0, kv_heads, ao_left, 0)
 
     @pl.when(has_next)
     def _():
@@ -375,7 +400,6 @@
     chunks = cols // width
     nt = rows // TILE
     slots = REACH * nh + 1
-    vmem = pl.BlockSpec(memory_space=pltpu.VMEM)
     dma = pltpu.SemaphoreType.DMA
     return pl.pallas_call(
         functools.partial(kernel, nz, nh, width),
@@ -384,8 +408,10 @@
             jax.ShapeDtypeStruct(queries.shape, BF16),
         ),
         in_specs=[pl.BlockSpec(memory_space=pltpu.HBM)] * 12,
-        out_specs=(vmem, vmem),
+        out_specs=(pl.BlockSpec(memory_space=pltpu.HBM),) * 2,
         scratch_shapes=[
+            pltpu.VMEM((rows, cols), BF16),
+            pltpu.VMEM(queries.shape, BF16),
             pltpu.SMEM(doc_lengths.shape, jnp.int32),
             pltpu.VMEM((rows, cols), BF16),
             pltpu.VMEM((rows, cols), BF16),
@@ -414,6 +440,8 @@
             pltpu.VMEM((kvw // HEAD_D, tok * queries.shape[1] // kvw, 1), F32),
             pltpu.VMEM((kvw // HEAD_D, tok * queries.shape[1] // kvw, 1), F32),
             dma((10 + 2 * (kvw // HEAD_D),)),
+            dma((chunks,)),
+            dma((kvw // HEAD_D,)),
             dma((slots, kvw // HEAD_D)),
             dma((2, kvw // HEAD_D)),
             dma((max(1, 4 * (nh - 1)), kvw // HEAD_D)),

time: 38.7 us -> 38.4 us (level)
  no operation moved by 1% of the time
where the time goes in v4:
time: 38.4 us; the launch traced here: 38.3 us
  Pallas kernels  34.5 us (90%)
  local copies, waits for them, and re-layouts  3.16 us (8%)
  between operations  0.65 us (2%)
    pallas_call x1, Pallas kernels, on_device(): pl.pallas_call(functools.partial(kernel, nz, nh, width), out_shape=(jax.S...  34.5 us
    unnamed x4, local copies, waits for them, and re-layouts  3.16 us

profile of v4, /device:TPU:24, one launch (start us, length us, event | category | flops | bytes accessed | tf_op | source)
XLA Modules:
  0.0 38.3 jit_solution(16963871900891279527)
XLA Ops:
  0.6 34.5 %shard_map.131 = (bf16[256,2048]{1,0:T(8,128)(2,1)}, bf16[128,2048]{1,0:T(8,128)(2,1)}) custom-call(s32[4]{0:T(128)} %dl_hbm.1, bf16[256,2048]{1,0:T(8,128)(2,1)} %x_hbm.1, bf16[256,2048]{1,0:T(8,128)(2,1)} %z_hbm.1, bf16[256,128]{1,0:T(8,128)(2,1)} %b_hbm.1, bf16[256,128]{1,0:T(8,128)(2,1)} %c_hbm.1, f32[32,256]{1,0:T(8,128)} %step_hbm.1, f32[1,32]{1,0:T(1,128)} %bitcast.4, ...), custom_call_target="tpu_custom_call" | custom-call | tf_op jit(solution)/shard_map/pallas_call | solution.py:404
  35.1 0.0 copy-start
  35.1 2.4 %copy.16 = bf16[256,2048]{1,0:T(8,128)(2,1)} copy(bf16[256,2048]{1,0:T(8,128)(2,1)} %get-tuple-element.4) | data formatting | bytes 2097152
  37.5 0.0 copy-done
  37.5 0.8 %copy.17 = bf16[128,2048]{1,0:T(8,128)(2,1)} copy(bf16[128,2048]{1,0:T(8,128)(2,1)S(1)} %copy-done) | data formatting | bytes 1048576
Async XLA Ops:
  35.1 2.4 %copy-start = (bf16[128,2048]{1,0:T(8,128)(2,1)S(1)}, bf16[128,2048]{1,0:T(8,128)(2,1)}, u32[]{:S(2)}) copy-start(bf16[128,2048]{1,0:T(8,128)(2,1)} %get-tuple-element.5) | copy-start | bytes 1572868
